TPU v7x, 512 devices: a whole 4x8x8 slice. The times are simulated.
512 devices in a mesh: dp: 16 (over y, core), attn: 32 (over x, z).
Axes of the slice: x: 4, y: 8, z: 8, core: 2. Of those that a mesh axis runs over, the one named last changes fastest.
Arguments:
- query_states: bfloat16 [65536, 4096], P(('dp', 'attn')), may hold values from -96 to 96
- key_states: bfloat16 [65536, 512], P(('dp', 'attn')), may hold values from -4.5 to 4.5
- value_states: bfloat16 [65536, 512], P(('dp', 'attn')), may hold values from -6 to 6
- out_grad: bfloat16 [65536, 4096], P(('dp', 'attn')), may hold values from -24 to 24
- doc_lengths: int32 [16, 12], P('dp'), may hold values from 1 to 384, 4096 in all within a row
- layer_inputs: bfloat16 [4096, 65536], P(None, ('dp', 'attn')), may hold values from -24 to 24
Outputs:
- query_grad: bfloat16 [65536, 4096], P(('dp', 'attn'))
- weight_grad: float32 [4096, 1024], P(('dp', 'attn'))
Inputs may be any that keep to these rules, and one draw needn't show every extreme that they name: `doc_lengths`: row g lists the lengths of the documents of data group g in the order in which they lie in its pack; they sum to 4096, and the longest is exactly 384.
All inputs are finite; a program needn't handle non-finite values.
Results may differ from a plain program's by a relative error of at most 0.0051.
Values may be sent and summed in bfloat16 or wider, within the bound.
A program may use at most 64 MiB of HBM per device.

v0:
```python
from functools import reduce

import jax
import jax.numpy as jnp
from jax import lax
from jax.sharding import PartitionSpec as P

DH = 128
SPAN = 3


masked_score = -1e30


def passed_along(shard, axis, by):
    size = lax.axis_size(axis)
    pairs = [(i, i + by) for i in range(size) if 0 <= i + by < size]
    return lax.ppermute(shard, axis, pairs)


def doc_index(position, bounds):
    return jnp.sum((position[:, None] >= bounds[None, :]).astype(jnp.int32), axis=1)


def fetch_direct(key_value, offset):
    return passed_along(key_value, "attn", offset)


def send_back(partial_value, offset):
    return passed_along(partial_value, "attn", -offset)


def row_adder(gathered, shard_rows):
    return jnp.dot(gathered, shard_rows, preferred_element_type=jnp.float32)


def shards(query_states, key_states, value_states, out_grad, doc_lengths, layer_inputs):
    rows_dev = query_states.shape[0]
    attn_size = lax.axis_size("attn")
    data_size = lax.axis_size("dp")
    key_width = key_states.shape[1]
    head_size = DH
    key_heads = key_width // head_size
    members = query_states.shape[1] // key_width
    score_scale = head_size ** (-0.5)
    device_rank = lax.axis_index("attn")
    query_pos = device_rank * rows_dev + jnp.arange(rows_dev, dtype=jnp.int32)
    bounds = jnp.cumsum(doc_lengths[0])
    query_doc = doc_index(query_pos, bounds)
    query_heads = query_states.reshape(rows_dev, key_heads, members, head_size)
    grad_heads = out_grad.reshape(rows_dev, key_heads, members, head_size)
    key_value = jnp.stack([key_states, value_states])
    blocks = [key_value]
    for offset in range(1, SPAN + 1):
        blocks.append(fetch_direct(key_value, offset))
    scores_all = []
    dprobs_all = []
    for offset in range(SPAN + 1):
        key_block = blocks[offset][0].reshape(rows_dev, key_heads, head_size)
        value_block = blocks[offset][1].reshape(rows_dev, key_heads, head_size)
        key_pos = query_pos - offset * rows_dev
        allowed = (key_pos[None, :] >= 0) & (key_pos[None, :] <= query_pos[:, None])
        allowed = allowed & (query_doc[:, None] == doc_index(key_pos, bounds)[None, :])
        scores = score_scale * jnp.einsum(
            "tgjd,ugd->gjtu", query_heads, key_block, preferred_element_type=jnp.float32
        )
        scores_all.append(jnp.where(allowed, scores, masked_score))
        dprobs_all.append(
            jnp.einsum(
                "tgjd,ugd->gjtu", grad_heads, value_block, preferred_element_type=jnp.float32
            )
        )
    row_max = reduce(
        jnp.maximum, [jnp.max(scores, axis=-1, keepdims=True) for scores in scores_all]
    )
    row_total = reduce(
        jnp.add,
        [jnp.sum(jnp.exp(scores - row_max), axis=-1, keepdims=True) for scores in scores_all],
    )
    row_delta = jnp.zeros_like(row_total)
    for offset in range(SPAN + 1):
        probs_block = jnp.exp(scores_all[offset] - row_max) / row_total
        row_delta = row_delta + jnp.sum(probs_block * dprobs_all[offset], axis=-1, keepdims=True)
    query_total = jnp.zeros((rows_dev, key_heads, members, head_size), jnp.float32)
    partials = []
    for offset in range(SPAN + 1):
        key_block = blocks[offset][0].reshape(rows_dev, key_heads, head_size)
        probs_block = jnp.exp(scores_all[offset] - row_max) / row_total
        dscores = (probs_block * (dprobs_all[offset] - row_delta)).astype(jnp.bfloat16)
        probs_low = probs_block.astype(jnp.bfloat16)
        query_total = query_total + jnp.einsum(
            "gjtu,ugd->tgjd", dscores, key_block, preferred_element_type=jnp.float32
        )
        key_part = score_scale * jnp.einsum(
            "gjtu,tgjd->ugd", dscores, query_heads, preferred_element_type=jnp.float32
        )
        value_part = jnp.einsum(
            "gjtu,tgjd->ugd", probs_low, grad_heads, preferred_element_type=jnp.float32
        )
        partials.append(jnp.stack([key_part, value_part]).reshape(2, rows_dev, key_width))
    query_grad = (
        (score_scale * query_total).astype(jnp.bfloat16).reshape(rows_dev, members * key_width)
    )
    grad_total = partials[0]
    for offset in range(1, SPAN + 1):
        grad_total = grad_total + send_back(partials[offset], offset)
    kv_rows = jnp.concatenate([grad_total[0], grad_total[1]], axis=1).astype(jnp.bfloat16)
    columns = kv_rows.shape[1]
    feat_size = layer_inputs.shape[0]
    norm_factor = float(rows_dev * attn_size * data_size) ** (-0.5)
    row_share = feat_size // (data_size * attn_size)
    viewed = layer_inputs.reshape(data_size, attn_size, row_share, rows_dev)
    gathered = lax.all_to_all(viewed, "attn", split_axis=1, concat_axis=3, tiled=True).reshape(
        data_size * row_share, attn_size * rows_dev
    )
    partial_term = row_adder(gathered, lax.all_gather(kv_rows, "attn", axis=0, tiled=True))
    summed = lax.psum_scatter(
        partial_term.reshape(data_size, row_share, columns), "dp", scatter_dimension=0, tiled=True
    )
    weight_grad = summed.reshape(-1, columns) * norm_factor
    return (query_grad, weight_grad)


def solution(mesh):
    placed = (
        P(("dp", "attn"), None),
        P(("dp", "attn"), None),
        P(("dp", "attn"), None),
        P(("dp", "attn"), None),
        P("dp", None),
        P(None, ("dp", "attn")),
    )
    return jax.shard_map(
        shards,
        mesh=mesh,
        in_specs=placed,
        out_specs=(P(("dp", "attn"), None), P(("dp", "attn"), None)),
        check_vma=False,
    )
```

profile of v0, /device:TPU:1, one launch (start us, length us, event | category | flops | bytes accessed | tf_op | source)
XLA Modules:
  0.0 333.7 jit_solution(5975572648770511432)
XLA Ops:
  7.2 1.2 copy.168
  8.4 1.0 copy.167
  10.2 7.3 %collective-permute-start.1 = (bf16[2,128,512]{1,2,0:T(8,128)(2,1)}, bf16[2,128,512]{1,2,0:T(8,128)(2,1)}, u32[]{:S(2)}, u32[]{:S(2)}) collective-permute-start(bf16[2,128,512]{1,2,0:T(8,128)(2,1)} %pad_maximum_fusion.3), channel_id=1, source_target_pairs={{0,2},{1,3},{2,4},{3,5},{4,6},{5,7},{6,8},{7,9},{8,10},{9,11},{10,... | collective-permute-start | bytes 786440 | tf_op jit(solution)/shard_map/ppermute | solution.py:18
  17.5 7.9 %collective-permute-start.2 = (bf16[2,128,512]{1,2,0:T(8,128)(2,1)}, bf16[2,128,512]{1,2,0:T(8,128)(2,1)}, u32[]{:S(2)}, u32[]{:S(2)}) collective-permute-start(bf16[2,128,512]{1,2,0:T(8,128)(2,1)} %pad_maximum_fusion.3), channel_id=1, source_target_pairs={{0,3},{1,4},{2,5},{3,6},{4,7},{5,8},{6,9},{7,10},{8,11},{9,12},{10... | collective-permute-start | bytes 786440 | tf_op jit(solution)/shard_map/ppermute | solution.py:18
  25.4 3.8 %collective-permute-start = (bf16[2,128,512]{1,2,0:T(8,128)(2,1)}, bf16[2,128,512]{1,2,0:T(8,128)(2,1)}, u32[]{:S(2)}, u32[]{:S(2)}) collective-permute-start(bf16[2,128,512]{1,2,0:T(8,128)(2,1)} %pad_maximum_fusion.3), channel_id=1, source_target_pairs={{0,1},{1,2},{2,3},{3,4},{4,5},{5,6},{6,7},{7,8},{8,9},{9,10},{10,1... | collective-permute-start | bytes 786440 | tf_op jit(solution)/shard_map/ppermute | solution.py:18
  36.6 15.5 %collective-permute-done = bf16[2,128,512]{1,2,0:T(8,128)(2,1)} collective-permute-done((bf16[2,128,512]{1,2,0:T(8,128)(2,1)}, bf16[2,128,512]{1,2,0:T(8,128)(2,1)}, u32[]{:S(2)}, u32[]{:S(2)}) %collective-permute-start) | collective-permute-done | bytes 262176 | tf_op jit(solution)/shard_map/ppermute | solution.py:18
  53.6 1.0 fusion.45
  55.1 1.0 fusion.47
  57.3 2.5 fusion.17
  62.4 2.4 fusion.8
  64.8 2.2 fusion.4
  67.6 1.3 collective-permute-start.5
  69.4 1.3 collective-permute-start.4
  71.2 1.5 collective-permute-start.3
  73.6 34.4 %collective-permute-done.5 = f32[2,128,512]{1,2,0:T(8,128)S(1)} collective-permute-done((f32[2,128,512]{1,2,0:T(8,128)S(1)}, f32[2,128,512]{1,2,0:T(8,128)S(1)}, u32[]{:S(2)}, u32[]{:S(2)}) %collective-permute-start.5) | collective-permute-done | bytes 524320 | tf_op jit(solution)/shard_map/ppermute | solution.py:18
  108.9 1.3 copy.204
  110.3 43.7 %all-to-all-start = ((bf16[16,32,8,128]{3,2,0,1:T(8,128)(2,1)}), bf16[16,32,8,128]{3,2,0,1:T(8,128)(2,1)S(1)}, u32[]{:S(2)}, u32[]{:S(2)}) async-start(bf16[16,32,8,128]{3,2,0,1:T(8,128)(2,1)} %copy.204), calls=%async_computation | async-start | bytes 2097152 | tf_op jit(solution)/shard_map/all_to_all | solution.py:113
  154.1 2.7 fusion.55
  156.8 26.4 %all-to-all-done = bf16[16,32,8,128]{3,2,0,1:T(8,128)(2,1)S(1)} async-done(((bf16[16,32,8,128]{3,2,0,1:T(8,128)(2,1)}), bf16[16,32,8,128]{3,2,0,1:T(8,128)(2,1)S(1)}, u32[]{:S(2)}, u32[]{:S(2)}) %all-to-all-start) | async-done | bytes 1048608 | tf_op jit(solution)/shard_map/all_to_all | solution.py:113
  183.8 77.4 %all-gather.2.cloned.1.call-done = bf16[4096,1024]{0,1:T(8,128)(2,1)} async-done(((bf16[128,1024]{0,1:T(8,128)(2,1)}), bf16[4096,1024]{0,1:T(8,128)(2,1)}) %all-gather.2.cloned.1.call-update) | async-done | bytes 8388624 | tf_op jit(solution)/shard_map/all_gather | solution.py:116
  261.3 7.2 %convolution_bitcast_fusion = f32[16,8,1024]{2,1,0:T(8,128)} fusion(bf16[4096,1024]{0,1:T(8,128)(2,1)} %all-gather.2.cloned.1.call-done, bf16[16,8,32,128]{3,2,1,0:T(8,128)(2,1)S(1)} %bitcast.249), kind=kOutput, calls=%fused_computation.41 | convolution fusion | flops 1073741824 | bytes 9961472 | tf_op jit(solution)/shard_map/dot_general | solution.py:34
  271.6 1.3 copy.206
  272.9 52.6 %reduce-scatter.2.cloned.1.call-done = f32[1,8,1024]{2,1,0:T(8,128)} async-done(((f32[16,8,1024]{2,1,0:T(8,128)}), f32[1,8,1024]{2,1,0:T(8,128)}) %reduce-scatter.2.cloned.1.call-update) | async-done | bytes 32784 | tf_op jit(solution)/shard_map/reduce_scatter | solution.py:117
  325.5 1.4 multiply_bitcast_fusion
  (72 shorter events, 20.7 us)
Async XLA Ops:
  7.2 25.1 %copy-start.8 = (bf16[128,4096]{1,0:T(8,128)(2,1)S(1)}, bf16[128,4096]{1,0:T(8,128)(2,1)}, u32[]{:S(2)}) copy-start(bf16[128,4096]{1,0:T(8,128)(2,1)} %param.9) | copy-start | bytes 3145732
  7.2 25.8 %copy-start.9 = (bf16[128,4096]{1,0:T(8,128)(2,1)S(1)}, bf16[128,4096]{1,0:T(8,128)(2,1)}, u32[]{:S(2)}) copy-start(bf16[128,4096]{1,0:T(8,128)(2,1)} %param.6) | copy-start | bytes 3145732
  7.2 254.1 %all-gather.2.cloned.1.call-start = ((), (), s32[]{:S(2)}) async-start(), calls=%async_computation.2 | async-start | bytes 8650752 | tf_op jit(solution)/shard_map/all_gather | solution.py:116
  10.2 45.0 %collective-permute-start.1 = (bf16[2,128,512]{1,2,0:T(8,128)(2,1)}, bf16[2,128,512]{1,2,0:T(8,128)(2,1)}, u32[]{:S(2)}, u32[]{:S(2)}) collective-permute-start(bf16[2,128,512]{1,2,0:T(8,128)(2,1)} %pad_maximum_fusion.3), channel_id=1, source_target_pairs={{0,2},{1,3},{2,4},{3,5},{4,6},{5,7},{6,8},{7,9},{8,10},{9,11},{10,... | collective-permute-start | bytes 786440 | tf_op jit(solution)/shard_map/ppermute | solution.py:18
  17.5 36.1 %collective-permute-start.2 = (bf16[2,128,512]{1,2,0:T(8,128)(2,1)}, bf16[2,128,512]{1,2,0:T(8,128)(2,1)}, u32[]{:S(2)}, u32[]{:S(2)}) collective-permute-start(bf16[2,128,512]{1,2,0:T(8,128)(2,1)} %pad_maximum_fusion.3), channel_id=1, source_target_pairs={{0,3},{1,4},{2,5},{3,6},{4,7},{5,8},{6,9},{7,10},{8,11},{9,12},{10... | collective-permute-start | bytes 786440 | tf_op jit(solution)/shard_map/ppermute | solution.py:18
  25.4 26.7 %collective-permute-start = (bf16[2,128,512]{1,2,0:T(8,128)(2,1)}, bf16[2,128,512]{1,2,0:T(8,128)(2,1)}, u32[]{:S(2)}, u32[]{:S(2)}) collective-permute-start(bf16[2,128,512]{1,2,0:T(8,128)(2,1)} %pad_maximum_fusion.3), channel_id=1, source_target_pairs={{0,1},{1,2},{2,3},{3,4},{4,5},{5,6},{6,7},{7,8},{8,9},{9,10},{10,1... | collective-permute-start | bytes 786440 | tf_op jit(solution)/shard_map/ppermute | solution.py:18
  56.1 0.6 copy-start.7
  67.0 2.3 copy-start.2
  67.1 2.3 copy-start.4
  67.1 3.6 %copy-start = (bf16[4,8,128,128]{2,3,1,0:T(8,128)(2,1)}, bf16[4,8,128,128]{2,3,1,0:T(8,128)(2,1)S(1)}, u32[]{:S(2)}) copy-start(bf16[4,8,128,128]{2,3,1,0:T(8,128)(2,1)S(1)} %get-tuple-element.33) | copy-start | bytes 3145732
  67.6 40.4 %collective-permute-start.5 = (f32[2,128,512]{1,2,0:T(8,128)S(1)}, f32[2,128,512]{1,2,0:T(8,128)S(1)}, u32[]{:S(2)}, u32[]{:S(2)}) collective-permute-start(f32[2,128,512]{1,2,0:T(8,128)S(1)} %pad_maximum_fusion.2), channel_id=1, source_target_pairs={{3,0},{4,1},{5,2},{6,3},{7,4},{8,5},{9,6},{10,7},{11,8},{12,9},{13... | collective-permute-start | bytes 1572872 | tf_op jit(solution)/shard_map/ppermute | solution.py:18
  69.4 38.6 %collective-permute-start.4 = (f32[2,128,512]{1,2,0:T(8,128)S(1)}, f32[2,128,512]{1,2,0:T(8,128)S(1)}, u32[]{:S(2)}, u32[]{:S(2)}) collective-permute-start(f32[2,128,512]{1,2,0:T(8,128)S(1)} %pad_maximum_fusion.1), channel_id=1, source_target_pairs={{2,0},{3,1},{4,2},{5,3},{6,4},{7,5},{8,6},{9,7},{10,8},{11,9},{12,... | collective-permute-start | bytes 1572872 | tf_op jit(solution)/shard_map/ppermute | solution.py:18
  71.2 36.9 %collective-permute-start.3 = (f32[2,128,512]{1,2,0:T(8,128)S(1)}, f32[2,128,512]{1,2,0:T(8,128)S(1)}, u32[]{:S(2)}, u32[]{:S(2)}) collective-permute-start(f32[2,128,512]{1,2,0:T(8,128)S(1)} %pad_maximum_fusion), channel_id=1, source_target_pairs={{1,0},{2,1},{3,2},{4,3},{5,4},{6,5},{7,6},{8,7},{9,8},{10,9},{11,1... | collective-permute-start | bytes 1572872 | tf_op jit(solution)/shard_map/ppermute | solution.py:18
  73.6 35.3 %copy-start.10 = (bf16[4096,128]{1,0:T(8,128)(2,1)S(1)}, bf16[4096,128]{1,0:T(8,128)(2,1)}, u32[]{:S(2)}) copy-start(bf16[4096,128]{1,0:T(8,128)(2,1)} %param.11) | copy-start | bytes 3145732
  108.9 45.2 %copy-start.3 = (bf16[4,8,128,128]{2,3,1,0:T(8,128)(2,1)S(1)}, bf16[4,8,128,128]{2,3,1,0:T(8,128)(2,1)}, u32[]{:S(2)}) copy-start(bf16[4,8,128,128]{2,3,1,0:T(8,128)(2,1)} %copy-done.2) | copy-start | bytes 3145732
  110.3 72.9 %all-to-all-start = ((bf16[16,32,8,128]{3,2,0,1:T(8,128)(2,1)}), bf16[16,32,8,128]{3,2,0,1:T(8,128)(2,1)S(1)}, u32[]{:S(2)}, u32[]{:S(2)}) async-start(bf16[16,32,8,128]{3,2,0,1:T(8,128)(2,1)} %copy.204), calls=%async_computation | async-start | bytes 2097152 | tf_op jit(solution)/shard_map/all_to_all | solution.py:113
  154.0 171.5 %reduce-scatter.2.cloned.1.call-start = ((), (), s32[]{:S(2)}) async-start(), calls=%async_computation.3 | async-start | bytes 557056 | tf_op jit(solution)/shard_map/reduce_scatter | solution.py:117
  261.3 7.2 %copy-start.1 = (bf16[4,8,128,128]{2,3,1,0:T(8,128)(2,1)S(1)}, bf16[4,8,128,128]{2,3,1,0:T(8,128)(2,1)}, u32[]{:S(2)}) copy-start(bf16[4,8,128,128]{2,3,1,0:T(8,128)(2,1)} %copy-done) | copy-start | bytes 3145732
  269.0 1.2 copy-start.5
  269.0 1.9 copy-start.6
Sparse Core Ops, SparseCore 0:
  109.0 152.2 all-gather.1
  268.6 56.8 reduce-scatter.1
where the time goes:
time: 335 us; the launch traced here: 334 us
  waiting for transfers between devices  206 us (61%)
  starting transfers between devices  66.9 us (20%)
  matrix products  21.1 us (6%)
  between operations  14.5 us (4%)
  local copies, waits for them, and re-layouts  14 us (4%)
  other arithmetic  10.8 us (3%)
    all_gather x1, waiting for transfers between devices, shards(): lax.all_gather(kv_rows, 'attn', axis=0, tiled=True)  77.4 us
    reduce_scatter x1, waiting for transfers between devices, shards(): lax.psum_scatter(partial_term.reshape(data_size, row_share, columns), 'dp...  52.6 us
    ppermute x6, waiting for transfers between devices, passed_along(): return lax.ppermute(shard, axis, pairs)  49.9 us
    all_to_all x1, starting transfers between devices, shards(): lax.all_to_all(viewed, 'attn', split_axis=1, concat_axis=3, tiled=True)  43.7 us
    all_to_all x1, waiting for transfers between devices, shards(): lax.all_to_all(viewed, 'attn', split_axis=1, concat_axis=3, tiled=True)  26.4 us
    ppermute x6, starting transfers between devices, passed_along(): return lax.ppermute(shard, axis, pairs)  23.1 us
    dot_general x1, matrix products, row_adder(): return jnp.dot(gathered, shard_rows, preferred_element_type=jnp.float32)  7.22 us
  transfers between devices with their start and end apart: 9, of which 5 were waited for; matrix products, arithmetic and copies ran while one was open for 6% of the time, Pallas kernels for 0%

commit v1 on v0

v1 whole, which is shorter than its diff:
```python
import functools

import jax
import jax.numpy as jnp
from jax import lax
from jax.experimental import pallas as pl
from jax.experimental.pallas import tpu as pltpu
from jax.sharding import PartitionSpec as P

DH = 128
SPAN = 3
NX, NY, NZ = 4, 8, 8
MEMBERS = 8
HEADS = 4
TOK = 128
LOG2E = 1.4426950408889634
HIDDEN = -1e30

IN0, IN1, IN2, ATT, OUT2, OUT3, OUT4, MUL, SUMY, SUMZ = range(10)
STEPS = HEADS + SUMZ


def kernel(
    doc_ref, q_ref, k_ref, v_ref, og_ref, x_ref, dq_ref, w_ref,
    kv, bias, probs, dscores, parts, osend, orecv, rows, xin, wsend, yrecv, zsend, zrecv,
    in_s, in_r, out_s, out_r, x_s, x_r, x_own, ag_s, ag_r, y_s, y_r, z_s, z_r,
):
    f32, bf16 = jnp.float32, jnp.bfloat16
    attn, dp = lax.axis_index("attn"), lax.axis_index("dp")
    x, z = attn // NZ, lax.rem(attn, NZ)
    y, core = dp // 2, lax.rem(dp, 2)
    right = (dp, lax.rem(attn + 1, NX * NZ))
    left = (dp, lax.rem(attn + NX * NZ - 1, NX * NZ))

    def in_team(r):
        c = lax.rem(core + r // NX, 2)
        return (y * 2 + c, lax.rem(x + lax.rem(r, NX), NX) * NZ + z)

    def in_y(s):
        return (lax.rem(y + s, NY) * 2 + core, attn)

    def in_z(s):
        return (dp, x * NZ + lax.rem(z + s, NZ))

    def remote(src, dst, send, recv, device):
        return pltpu.make_async_remote_copy(
            src_ref=src, dst_ref=dst, send_sem=send, recv_sem=recv,
            device_id=device, device_id_type=pl.DeviceIdType.MESH,
        )

    def arrived(ref, sem):
        pltpu.make_async_copy(ref, ref, sem).wait()

    barrier = pltpu.get_barrier_semaphore()

    def greet(device):
        pl.semaphore_signal(barrier, inc=1, device_id=device, device_id_type=pl.DeviceIdType.MESH)

    greet(right)
    greet(left)

    def greet_all(s, carry):
        greet(in_team(s))
        greet(in_y(s))
        greet(in_z(s))
        return carry

    lax.fori_loop(1, 8, greet_all, 0)

    for g in range(HEADS):
        kv[g, 0, 0] = k_ref[:, g * DH:(g + 1) * DH]
        kv[g, 0, 1] = v_ref[:, g * DH:(g + 1) * DH]

    query_pos = attn * TOK + lax.broadcasted_iota(jnp.int32, (1, TOK), 1)
    first = jnp.zeros((1, TOK), jnp.int32)
    bound = jnp.int32(0)
    for c in range(doc_ref.shape[1]):
        bound = bound + doc_ref[0, c]
        first = jnp.where(query_pos >= bound, bound, first)
    for o in range(SPAN + 1):
        key_pos = (attn - o) * TOK + lax.broadcasted_iota(jnp.int32, (TOK, TOK), 0)
        seen = (key_pos >= first) & (key_pos <= query_pos)
        bias[o * TOK:(o + 1) * TOK] = jnp.where(seen, 0.0, HIDDEN)

    pl.semaphore_wait(barrier, 2 + 7 * 3)

    def at(t, delay, body):
        g = t - delay
        pl.when((g >= 0) & (g < HEADS))(lambda: body(jnp.clip(g, 0, HEADS - 1)))

    def pass_in(g, o):
        return remote(kv.at[g, o], kv.at[g, o + 1], in_s.at[g, o], in_r.at[g, o], right)

    def pass_out(g, o):
        return remote(osend.at[g, o], orecv.at[g, o], out_s.at[g, o], out_r.at[g, o], left)

    def share_x(r):
        return remote(x_ref.at[:, in_slot(r)], xin.at[r], x_s.at[r], x_r.at[r], in_team(r))

    def in_slot(r):
        return lax.rem(core + r // NX, 2) * NX + lax.rem(x + lax.rem(r, NX), NX)

    own_x = pltpu.make_async_copy(x_ref.at[:, in_slot(0)], xin.at[0], x_own)

    def do_in0(g):
        pass_in(g, 0).start()

    def do_in1(g):
        pass_in(g, 0).wait_recv()
        pass_in(g, 1).start()

    def do_in2(g):
        pass_in(g, 1).wait_recv()
        pass_in(g, 2).start()

    def nt(a, b):
        return lax.dot_general(a, b, (((1,), (1,)), ((), ())), preferred_element_type=f32)

    def do_att(g):
        pass_in(g, 2).wait_recv()
        keys = kv[g, :, 0].reshape(4 * TOK, DH)
        values = kv[g, :, 1].reshape(4 * TOK, DH)
        group = pl.ds(pl.multiple_of(g * MEMBERS * DH, DH), MEMBERS * DH)

        def member(j, carry):
            cols = pl.ds(pl.multiple_of((g * MEMBERS + j) * DH, DH), DH)
            scores = nt(keys, q_ref[:, cols]) + bias[...]
            dprobs = nt(values, og_ref[:, cols])
            top = jnp.max(scores, axis=0, keepdims=True)
            weights = jnp.exp2((scores - top) * (LOG2E * DH ** -0.5))
            p = weights * (1.0 / jnp.sum(weights, axis=0, keepdims=True))
            delta = jnp.sum(p * dprobs, axis=0, keepdims=True)
            spot = pl.ds(pl.multiple_of(j * TOK, TOK), TOK)
            probs[:, spot] = p.astype(bf16)
            dscores[:, spot] = (p * (dprobs - delta)).astype(bf16)
            return carry

        lax.fori_loop(0, MEMBERS, member, 0)
        ds = dscores[...]

        def stacked(ref):
            wide = ref[:, group]
            return jnp.concatenate([wide[:, j * DH:(j + 1) * DH] for j in range(MEMBERS)], axis=0)

        dk = jnp.dot(ds, stacked(q_ref), preferred_element_type=f32) * (DH ** -0.5)
        dv = jnp.dot(probs[...], stacked(og_ref), preferred_element_type=f32)
        for o in range(SPAN + 1):
            parts[g, o, :, :DH] = dk[o * TOK:(o + 1) * TOK]
            parts[g, o, :, DH:] = dv[o * TOK:(o + 1) * TOK]
        osend[g, 0] = parts[g, SPAN].astype(bf16)
        pass_out(g, 0).start()
        dqt = jnp.dot(keys.T, ds, preferred_element_type=f32) * (DH ** -0.5)
        dq_ref[:, group] = jnp.concatenate(
            [dqt[:, j * TOK:(j + 1) * TOK].T for j in range(MEMBERS)], axis=1
        ).astype(bf16)

    def do_out2(g):
        pass_out(g, 0).wait_recv()
        osend[g, 1] = (orecv[g, 0].astype(f32) + parts[g, 2]).astype(bf16)
        pass_out(g, 1).start()

    def do_out3(g):
        pass_out(g, 1).wait_recv()
        osend[g, 2] = (orecv[g, 1].astype(f32) + parts[g, 1]).astype(bf16)
        pass_out(g, 2).start()

    def share_rows(g, r):
        return remote(rows.at[g, 0], rows.at[g, r], ag_s.at[g], ag_r.at[g], in_team(r))

    def do_out4(g):
        pass_out(g, 2).wait_recv()
        rows[g, 0] = (orecv[g, 2].astype(f32) + parts[g, 0]).astype(bf16)

        def send(r, carry):
            share_rows(g, r).start()
            return carry

        lax.fori_loop(1, 8, send, 0)

    def share_y(g, s):
        return remote(
            wsend.at[g, lax.rem(y + s, NY)], yrecv.at[g, s - 1], y_s.at[g], y_r.at[g], in_y(s)
        )

    def do_mul(g):
        arrived(rows.at[g, pl.ds(1, 7)], ag_r.at[g])
        taken = jnp.concatenate(
            [xin[r].reshape(NY * 64, TOK) for r in range(8)], axis=1
        )
        out = jnp.dot(taken, rows[g].reshape(8 * TOK, 2 * DH), preferred_element_type=f32)
        wsend[g] = out.astype(bf16).reshape(NY, 64, 2 * DH)

        def send(s, carry):
            share_y(g, s).start()
            return carry

        lax.fori_loop(1, NY, send, 0)

    def share_z(g, s):
        return remote(
            zsend.at[g, lax.rem(z + s, NZ)], zrecv.at[g, s - 1], z_s.at[g], z_r.at[g], in_z(s)
        )

    def do_sumy(g):
        arrived(yrecv.at[g], y_r.at[g])
        total = wsend[g, y].astype(f32)
        for s in range(NY - 1):
            total = total + yrecv[g, s].astype(f32)
        zsend[g] = total.reshape(NZ, 8, 2 * DH)

        def send(s, carry):
            share_z(g, s).start()
            return carry

        lax.fori_loop(1, NZ, send, 0)

    norm = (NX * NY * NZ * 2 * TOK) ** -0.5

    def do_sumz(g):
        arrived(zrecv.at[g], z_r.at[g])
        total = zsend[g, z]
        for s in range(NZ - 1):
            total = total + zrecv[g, s]
        total = total * norm
        w_ref[:, pl.ds(pl.multiple_of(g * DH, DH), DH)] = total[:, :DH]
        w_ref[:, pl.ds(pl.multiple_of((HEADS + g) * DH, DH), DH)] = total[:, DH:]

    def step(t, carry):
        at(t, IN0, do_in0)

        @pl.when(t == 0)
        def _():
            own_x.start()

            def send(r, inner):
                share_x(r).start()
                return inner

            lax.fori_loop(1, 8, send, 0)

        at(t, IN1, do_in1)
        at(t, IN2, do_in2)
        at(t, SUMZ, do_sumz)
        at(t, SUMY, do_sumy)

        @pl.when(t == MUL)
        def _():
            own_x.wait()

            def receive(r, inner):
                share_x(r).wait_recv()
                return inner

            lax.fori_loop(1, 8, receive, 0)

        at(t, MUL, do_mul)
        at(t, OUT4, do_out4)
        at(t, OUT3, do_out3)
        at(t, OUT2, do_out2)
        at(t, ATT, do_att)
        return carry

    lax.fori_loop(0, STEPS, step, 0)

    def sent_x(r, carry):
        share_x(r).wait_send()
        return carry

    lax.fori_loop(1, 8, sent_x, 0)

    def sent(g, carry):
        for o in range(SPAN):
            pass_in(g, o).wait_send()
            pass_out(g, o).wait_send()
        arrived(rows.at[g, pl.ds(1, 7)], ag_s.at[g])
        arrived(yrecv.at[g], y_s.at[g])
        arrived(zrecv.at[g], z_s.at[g])
        return carry

    lax.fori_loop(0, HEADS, sent, 0)


def shards(query_states, key_states, value_states, out_grad, doc_lengths, layer_inputs):
    rows_dev, width = query_states.shape
    columns = 2 * key_states.shape[1]
    team = 2 * NX
    by_row = layer_inputs.reshape(NY, team, layer_inputs.shape[0] // (NY * team), rows_dev)
    bf16, f32 = jnp.bfloat16, jnp.float32
    vmem = pl.BlockSpec(memory_space=pltpu.VMEM)
    dma = pltpu.SemaphoreType.DMA
    return pl.pallas_call(
        kernel,
        out_shape=(
            jax.ShapeDtypeStruct((rows_dev, width), bf16),
            jax.ShapeDtypeStruct((8, columns), f32),
        ),
        in_specs=[
            pl.BlockSpec(memory_space=pltpu.SMEM), vmem, vmem, vmem, vmem,
            pl.BlockSpec(memory_space=pl.ANY),
        ],
        out_specs=(vmem, vmem),
        scratch_shapes=[
            pltpu.VMEM((HEADS, SPAN + 1, 2, TOK, DH), bf16),
            pltpu.VMEM((4 * TOK, TOK), f32),
            pltpu.VMEM((4 * TOK, MEMBERS * TOK), bf16),
            pltpu.VMEM((4 * TOK, MEMBERS * TOK), bf16),
            pltpu.VMEM((HEADS, SPAN + 1, TOK, 2 * DH), f32),
            pltpu.VMEM((HEADS, SPAN, TOK, 2 * DH), bf16),
            pltpu.VMEM((HEADS, SPAN, TOK, 2 * DH), bf16),
            pltpu.VMEM((HEADS, 8, TOK, 2 * DH), bf16),
            pltpu.VMEM((8, NY, 64, TOK), bf16),
            pltpu.VMEM((HEADS, NY, 64, 2 * DH), bf16),
            pltpu.VMEM((HEADS, NY - 1, 64, 2 * DH), bf16),
            pltpu.VMEM((HEADS, NZ, 8, 2 * DH), f32),
            pltpu.VMEM((HEADS, NZ - 1, 8, 2 * DH), f32),
            dma((HEADS, SPAN)), dma((HEADS, SPAN)),
            dma((HEADS, SPAN)), dma((HEADS, SPAN)),
            dma((8,)), dma((8,)), dma,
            dma((HEADS,)), dma((HEADS,)),
            dma((HEADS,)), dma((HEADS,)),
            dma((HEADS,)), dma((HEADS,)),
        ],
        compiler_params=pltpu.CompilerParams(
            collective_id=0, has_side_effects=True, vmem_limit_bytes=44 << 20
        ),
        name="attention_and_weight_grad",
    )(doc_lengths, query_states, key_states, value_states, out_grad, by_row)


def solution(mesh):
    whole = P(("dp", "attn"), None)
    return jax.shard_map(
        shards,
        mesh=mesh,
        in_specs=(whole, whole, whole, whole, P("dp", None), P(None, ("dp", "attn"))),
        out_specs=(whole, whole),
        check_vma=False,
    )
```

time: 335 us -> 112 us (0.33)
  waiting for transfers between devices: 206 us -> 0 us
  Pallas kernels: 0 us -> 103 us
  starting transfers between devices: 66.9 us -> 0 us
  matrix products: 21.1 us -> 0 us
  between operations: 14.5 us -> 0.65 us
  other arithmetic: 10.8 us -> 0 us
  local copies, waits for them, and re-layouts: 14 us -> 7.72 us
    pallas_call x0 -> x1, Pallas kernels: none -> 103 us  [shards(): pl.pallas_call(kernel, out_shape=(jax.ShapeDtypeStruct((rows_dev, width),...]
    all_gather x1 -> x0, waiting for transfers between devices: 77.4 us -> none  [shards(): lax.all_gather(kv_rows, 'attn', axis=0, tiled=True)]
    reduce_scatter x1 -> x0, waiting for transfers between devices: 52.6 us -> none  [shards(): lax.psum_scatter(partial_term.reshape(data_size, row_share, columns), 'dp...]
    ppermute x6 -> x0, waiting for transfers between devices: 49.9 us -> none  [passed_along(): return lax.ppermute(shard, axis, pairs)]
    all_to_all x1 -> x0, starting transfers between devices: 43.7 us -> none  [shards(): lax.all_to_all(viewed, 'attn', split_axis=1, concat_axis=3, tiled=True)]
    all_to_all x1 -> x0, waiting for transfers between devices: 26.4 us -> none  [shards(): lax.all_to_all(viewed, 'attn', split_axis=1, concat_axis=3, tiled=True)]
    ppermute x6 -> x0, starting transfers between devices: 23.1 us -> none  [passed_along(): return lax.ppermute(shard, axis, pairs)]
    dot_general x21 -> x0, matrix products: 21.1 us -> none  [the longest x1 7.22 us: row_adder(): return jnp.dot(gathered, shard_rows, preferred_element_type=jnp.float32)]
  transfers between devices with their start and end apart: 9 -> 0, of which waited for: 5 -> 0; matrix products, arithmetic and copies ran while one was open for 6% -> 0% of each run, Pallas kernels for 0% -> 0%
where the time goes in v1:
time: 112 us
  Pallas kernels  103 us (92%)
  local copies, waits for them, and re-layouts  7.72 us (7%)
    pallas_call x1, Pallas kernels, shards(): pl.pallas_call(kernel, out_shape=(jax.ShapeDtypeStruct((rows_dev, width),...  103 us
    unnamed x14, local copies, waits for them, and re-layouts  7.72 us

profile of v1, /device:TPU:1, one launch (start us, length us, event | category | flops | bytes accessed | tf_op | source)
XLA Modules:
  0.0 111.8 jit_solution(1815464637134598802)
XLA Ops:
  0.6 0.0 copy-start.5
  0.6 0.6 copy-done.5
  1.3 0.0 copy-start
  1.3 1.2 %copy-done = bf16[128,4096]{1,0:T(8,128)(2,1)S(1)} copy-done((bf16[128,4096]{1,0:T(8,128)(2,1)S(1)}, bf16[128,4096]{1,0:T(8,128)(2,1)}, u32[]{:S(2)}) %copy-start) | copy-done | bytes 1048600
  2.5 0.0 copy-start.1
  2.5 1.2 %copy-done.1 = bf16[128,4096]{1,0:T(8,128)(2,1)S(1)} copy-done((bf16[128,4096]{1,0:T(8,128)(2,1)S(1)}, bf16[128,4096]{1,0:T(8,128)(2,1)}, u32[]{:S(2)}) %copy-start.1) | copy-done | bytes 1048600
  3.7 0.0 copy-start.2
  3.7 1.2 %copy-done.2 = bf16[4096,128]{1,0:T(8,128)(2,1)S(1)} copy-done((bf16[4096,128]{1,0:T(8,128)(2,1)S(1)}, bf16[4096,128]{1,0:T(8,128)(2,1)}, u32[]{:S(2)}) %copy-start.2) | copy-done | bytes 1048600
  5.0 0.0 copy-start.3
  5.0 0.9 copy-done.3
  5.9 0.0 copy-start.4
  5.9 0.9 copy-done.4
  6.8 103.4 %attention_and_weight_grad.1 = (bf16[128,4096]{1,0:T(8,128)(2,1)S(1)}, f32[8,1024]{1,0:T(8,128)S(1)}) custom-call(s32[1,12]{1,0:T(1,128)S(1)} %copy-done.5, bf16[128,4096]{1,0:T(8,128)(2,1)S(1)} %copy-done, bf16[128,512]{1,0:T(8,128)(2,1)S(1)} %copy-done.3, bf16[128,512]{1,0:T(8,128)(2,1)S(1)} %copy-done.4, bf16[128,4096]{1,0:T(8,128)(2,1)S(1)} %copy-done.1, ...), custom_call_target="tpu_custom_call" | custom-call | tf_op jit(solution)/shard_map/attention_and_weight_grad/pallas_call | solution.py:291
  110.2 1.0 copy.10
  111.1 0.6 copy.11
Async XLA Ops:
  0.6 0.7 copy-start.5
  1.3 1.2 %copy-start = (bf16[128,4096]{1,0:T(8,128)(2,1)S(1)}, bf16[128,4096]{1,0:T(8,128)(2,1)}, u32[]{:S(2)}) copy-start(bf16[128,4096]{1,0:T(8,128)(2,1)} %q_ref.1) | copy-start | bytes 3145732
  2.5 1.2 %copy-start.1 = (bf16[128,4096]{1,0:T(8,128)(2,1)S(1)}, bf16[128,4096]{1,0:T(8,128)(2,1)}, u32[]{:S(2)}) copy-start(bf16[128,4096]{1,0:T(8,128)(2,1)} %og_ref.1) | copy-start | bytes 3145732
  3.7 1.2 %copy-start.2 = (bf16[4096,128]{1,0:T(8,128)(2,1)S(1)}, bf16[4096,128]{1,0:T(8,128)(2,1)}, u32[]{:S(2)}) copy-start(bf16[4096,128]{1,0:T(8,128)(2,1)} %param.11) | copy-start | bytes 3145732
  5.0 0.9 copy-start.3
  5.9 0.9 copy-start.4

commit v2 on v1

--- a/solution.py
+++ b/solution.py
@@ -16,14 +16,15 @@
 LOG2E = 1.4426950408889634
 HIDDEN = -1e30
 
-IN0, IN1, IN2, ATT, OUT2, OUT3, OUT4, MUL, SUMY, SUMZ = range(10)
-STEPS = HEADS + SUMZ
+IN0, IN1, IN2, ATT, OUT2, OUT3, OUT4, MUL, SUMY, SUMZ = 0, 1, 2, 3, 5, 6, 7, 9, 12, 14
+STEPS = 2 * HEADS - 1 + SUMZ
+HALF = MEMBERS // 2
 
 
 def kernel(
-    doc_ref, q_ref, k_ref, v_ref, og_ref, x_ref, dq_ref, w_ref,
-    kv, bias, probs, dscores, parts, osend, orecv, rows, xin, wsend, yrecv, zsend, zrecv,
-    in_s, in_r, out_s, out_r, x_s, x_r, x_own, ag_s, ag_r, y_s, y_r, z_s, z_r,
+    doc_hbm, q_hbm, k_hbm, v_hbm, og_hbm, x_ref, dq_hbm, w_ref,
+    doc_ref, q_ref, og_ref, dq_ref, kv, bias, parts, osend, orecv, rows, xin, wsend, yrecv, zsend, zrecv,
+    load_s, kv_s, dq_s, in_s, in_r, out_s, out_r, x_s, x_r, x_own, ag_s, ag_r, y_s, y_r, z_s, z_r,
 ):
     f32, bf16 = jnp.float32, jnp.bfloat16
     attn, dp = lax.axis_index("attn"), lax.axis_index("dp")
@@ -51,6 +52,25 @@
     def arrived(ref, sem):
         pltpu.make_async_copy(ref, ref, sem).wait()
 
+    loads = [
+        pltpu.make_async_copy(src, dst, load_s.at[i])
+        for i, (src, dst) in enumerate(((doc_hbm, doc_ref), (q_hbm, q_ref), (og_hbm, og_ref)))
+    ]
+
+    def own_kv(g):
+        cols = pl.ds(pl.multiple_of(g * DH, DH), DH)
+        return [
+            pltpu.make_async_copy(src.at[:, cols], kv.at[g, 0, i], kv_s.at[g, i])
+            for i, src in enumerate((k_hbm, v_hbm))
+        ]
+
+    loads[0].start()
+    for g in range(HEADS):
+        for copy in own_kv(g):
+            copy.start()
+    loads[1].start()
+    loads[2].start()
+
     barrier = pltpu.get_barrier_semaphore()
 
     def greet(device):
@@ -67,10 +87,7 @@
 
     lax.fori_loop(1, 8, greet_all, 0)
 
-    for g in range(HEADS):
-        kv[g, 0, 0] = k_ref[:, g * DH:(g + 1) * DH]
-        kv[g, 0, 1] = v_ref[:, g * DH:(g + 1) * DH]
-
+    loads[0].wait()
     query_pos = attn * TOK + lax.broadcasted_iota(jnp.int32, (1, TOK), 1)
     first = jnp.zeros((1, TOK), jnp.int32)
     bound = jnp.int32(0)
@@ -85,8 +102,9 @@
     pl.semaphore_wait(barrier, 2 + 7 * 3)
 
     def at(t, delay, body):
-        g = t - delay
-        pl.when((g >= 0) & (g < HEADS))(lambda: body(jnp.clip(g, 0, HEADS - 1)))
+        late = t - delay
+        due = (late >= 0) & (late < 2 * HEADS) & (lax.rem(late + 2, 2) == 0)
+        pl.when(due)(lambda: body(jnp.clip(late // 2, 0, HEADS - 1)))
 
     def pass_in(g, o):
         return remote(kv.at[g, o], kv.at[g, o + 1], in_s.at[g, o], in_r.at[g, o], right)
@@ -103,6 +121,8 @@
     own_x = pltpu.make_async_copy(x_ref.at[:, in_slot(0)], xin.at[0], x_own)
 
     def do_in0(g):
+        for copy in own_kv(g):
+            copy.wait()
         pass_in(g, 0).start()
 
     def do_in1(g):
@@ -116,43 +136,54 @@
     def nt(a, b):
         return lax.dot_general(a, b, (((1,), (1,)), ((), ())), preferred_element_type=f32)
 
-    def do_att(g):
-        pass_in(g, 2).wait_recv()
+    def leave_dq(g, half):
+        cols = pl.ds(pl.multiple_of((g * MEMBERS + half * HALF) * DH, HALF * DH), HALF * DH)
+        return pltpu.make_async_copy(dq_ref.at[:, cols], dq_hbm.at[:, cols], dq_s.at[g, half])
+
+    def do_att(g, half):
         keys = kv[g, :, 0].reshape(4 * TOK, DH)
         values = kv[g, :, 1].reshape(4 * TOK, DH)
-        group = pl.ds(pl.multiple_of(g * MEMBERS * DH, DH), MEMBERS * DH)
-
-        def member(j, carry):
-            cols = pl.ds(pl.multiple_of((g * MEMBERS + j) * DH, DH), DH)
-            scores = nt(keys, q_ref[:, cols]) + bias[...]
-            dprobs = nt(values, og_ref[:, cols])
+        base = (g * MEMBERS + half * HALF) * DH
+        group = pl.ds(pl.multiple_of(base, HALF * DH), HALF * DH)
+
+        def heads_of(ref):
+            wide = ref[:, group]
+            return [wide[:, j * DH:(j + 1) * DH] for j in range(HALF)]
+
+        queries, grads = heads_of(q_ref), heads_of(og_ref)
+        low_probs, dscores = [], []
+        for j in range(HALF):
+            scores = nt(keys, queries[j]) + bias[...]
+            dprobs = nt(values, grads[j])
             top = jnp.max(scores, axis=0, keepdims=True)
             weights = jnp.exp2((scores - top) * (LOG2E * DH ** -0.5))
             p = weights * (1.0 / jnp.sum(weights, axis=0, keepdims=True))
             delta = jnp.sum(p * dprobs, axis=0, keepdims=True)
-            spot = pl.ds(pl.multiple_of(j * TOK, TOK), TOK)
-            probs[:, spot] = p.astype(bf16)
-            dscores[:, spot] = (p * (dprobs - delta)).astype(bf16)
-            return carry
-
-        lax.fori_loop(0, MEMBERS, member, 0)
-        ds = dscores[...]
-
-        def stacked(ref):
-            wide = ref[:, group]
-            return jnp.concatenate([wide[:, j * DH:(j + 1) * DH] for j in range(MEMBERS)], axis=0)
-
-        dk = jnp.dot(ds, stacked(q_ref), preferred_element_type=f32) * (DH ** -0.5)
-        dv = jnp.dot(probs[...], stacked(og_ref), preferred_element_type=f32)
-        for o in range(SPAN + 1):
-            parts[g, o, :, :DH] = dk[o * TOK:(o + 1) * TOK]
-            parts[g, o, :, DH:] = dv[o * TOK:(o + 1) * TOK]
-        osend[g, 0] = parts[g, SPAN].astype(bf16)
-        pass_out(g, 0).start()
+            low_probs.append(p.astype(bf16))
+            dscores.append((p * (dprobs - delta)).astype(bf16))
+        ds = jnp.concatenate(dscores, axis=1)
+        dk = jnp.dot(ds, jnp.concatenate(queries, axis=0), preferred_element_type=f32)
+        dv = jnp.dot(
+            jnp.concatenate(low_probs, axis=1), jnp.concatenate(grads, axis=0),
+            preferred_element_type=f32,
+        )
+        new = jnp.concatenate([dk * (DH ** -0.5), dv], axis=1).reshape(SPAN + 1, TOK, 2 * DH)
         dqt = jnp.dot(keys.T, ds, preferred_element_type=f32) * (DH ** -0.5)
         dq_ref[:, group] = jnp.concatenate(
-            [dqt[:, j * TOK:(j + 1) * TOK].T for j in range(MEMBERS)], axis=1
+            [dqt[:, j * TOK:(j + 1) * TOK].T for j in range(HALF)], axis=1
         ).astype(bf16)
+        leave_dq(g, half).start()
+
+        @pl.when(half == 0)
+        def _():
+            parts[g] = new
+
+        @pl.when(half == 1)
+        def _():
+            total = parts[g] + new
+            parts[g] = total
+            osend[g, 0] = total[SPAN].astype(bf16)
+            pass_out(g, 0).start()
 
     def do_out2(g):
         pass_out(g, 0).wait_recv()
@@ -240,8 +271,9 @@
 
         at(t, IN1, do_in1)
         at(t, IN2, do_in2)
-        at(t, SUMZ, do_sumz)
-        at(t, SUMY, do_sumy)
+        at(t, OUT2, do_out2)
+        at(t, OUT3, do_out3)
+        at(t, OUT4, do_out4)
 
         @pl.when(t == MUL)
         def _():
@@ -254,10 +286,27 @@
             lax.fori_loop(1, 8, receive, 0)
 
         at(t, MUL, do_mul)
-        at(t, OUT4, do_out4)
-        at(t, OUT3, do_out3)
-        at(t, OUT2, do_out2)
-        at(t, ATT, do_att)
+        at(t, SUMY, do_sumy)
+        at(t, SUMZ, do_sumz)
+
+        @pl.when(t == ATT)
+        def _():
+            loads[1].wait()
+            loads[2].wait()
+
+        late = t - ATT
+
+        @pl.when((late >= 0) & (late < 2 * HEADS))
+        def _():
+            g = jnp.clip(late // 2, 0, HEADS - 1)
+            half = lax.rem(late + 2, 2)
+
+            @pl.when(half == 0)
+            def _():
+                pass_in(g, 2).wait_recv()
+
+            do_att(g, half)
+
         return carry
 
     lax.fori_loop(0, STEPS, step, 0)
@@ -275,6 +324,8 @@
         arrived(rows.at[g, pl.ds(1, 7)], ag_s.at[g])
         arrived(yrecv.at[g], y_s.at[g])
         arrived(zrecv.at[g], z_s.at[g])
+        leave_dq(g, 0).wait()
+        leave_dq(g, 1).wait()
         return carry
 
     lax.fori_loop(0, HEADS, sent, 0)
@@ -294,16 +345,15 @@
             jax.ShapeDtypeStruct((rows_dev, width), bf16),
             jax.ShapeDtypeStruct((8, columns), f32),
         ),
-        in_specs=[
-            pl.BlockSpec(memory_space=pltpu.SMEM), vmem, vmem, vmem, vmem,
-            pl.BlockSpec(memory_space=pl.ANY),
-        ],
-        out_specs=(vmem, vmem),
+        in_specs=[pl.BlockSpec(memory_space=pltpu.HBM)] * 6,
+        out_specs=(pl.BlockSpec(memory_space=pltpu.HBM), vmem),
         scratch_shapes=[
+            pltpu.SMEM(doc_lengths.shape, jnp.int32),
+            pltpu.VMEM((rows_dev, width), bf16),
+            pltpu.VMEM((rows_dev, width), bf16),
+            pltpu.VMEM((rows_dev, width), bf16),
             pltpu.VMEM((HEADS, SPAN + 1, 2, TOK, DH), bf16),
             pltpu.VMEM((4 * TOK, TOK), f32),
-            pltpu.VMEM((4 * TOK, MEMBERS * TOK), bf16),
-            pltpu.VMEM((4 * TOK, MEMBERS * TOK), bf16),
             pltpu.VMEM((HEADS, SPAN + 1, TOK, 2 * DH), f32),
             pltpu.VMEM((HEADS, SPAN, TOK, 2 * DH), bf16),
             pltpu.VMEM((HEADS, SPAN, TOK, 2 * DH), bf16),
@@ -313,6 +363,7 @@
             pltpu.VMEM((HEADS, NY - 1, 64, 2 * DH), bf16),
             pltpu.VMEM((HEADS, NZ, 8, 2 * DH), f32),
             pltpu.VMEM((HEADS, NZ - 1, 8, 2 * DH), f32),
+            dma((3,)), dma((HEADS, 2)), dma((HEADS, 2)),
             dma((HEADS, SPAN)), dma((HEADS, SPAN)),
             dma((HEADS, SPAN)), dma((HEADS, SPAN)),
             dma((8,)), dma((8,)), dma,
@@ -321,7 +372,7 @@
             dma((HEADS,)), dma((HEADS,)),
         ],
         compiler_params=pltpu.CompilerParams(
-            collective_id=0, has_side_effects=True, vmem_limit_bytes=44 << 20
+            collective_id=0, has_side_effects=True, vmem_limit_bytes=62 << 20
         ),
         name="attention_and_weight_grad",
     )(doc_lengths, query_states, key_states, value_states, out_grad, by_row)

time: 112 us -> 93.2 us (0.83)
  Pallas kernels: 103 us -> 89.3 us
  local copies, waits for them, and re-layouts: 7.72 us -> 2.91 us
    pallas_call x1, Pallas kernels: 103 us -> 89.3 us  [shards(): pl.pallas_call(kernel, out_shape=(jax.ShapeDtypeStruct((rows_dev, width),...]
    unnamed x14 -> x4, local copies, waits for them, and re-layouts: 7.72 us -> 2.91 us
where the time goes in v2:
time: 93.2 us; the launch traced here: 92.9 us
  Pallas kernels  89.3 us (96%)
  local copies, waits for them, and re-layouts  2.91 us (3%)
    pallas_call x1, Pallas kernels, shards(): pl.pallas_call(kernel, out_shape=(jax.ShapeDtypeStruct((rows_dev, width),...  89.3 us
    unnamed x4, local copies, waits for them, and re-layouts  2.91 us

profile of v2, /device:TPU:1, one launch (start us, length us, event | category | flops | bytes accessed | tf_op | source)
XLA Modules:
  0.0 92.9 jit_solution(3435619905273258710)
XLA Ops:
  0.6 89.3 %attention_and_weight_grad.1 = (bf16[128,4096]{1,0:T(8,128)(2,1)}, f32[8,1024]{1,0:T(8,128)}) custom-call(s32[1,12]{1,0:T(1,128)} %doc_hbm.1, bf16[128,4096]{1,0:T(8,128)(2,1)} %q_hbm.1, bf16[128,512]{1,0:T(8,128)(2,1)} %k_hbm.1, bf16[128,512]{1,0:T(8,128)(2,1)} %v_hbm.1, bf16[128,4096]{1,0:T(8,128)(2,1)} %og_hbm.1, bf16[8,8,64,128]{3,2,1,0:T(8,128)(2,1)} %bitcast.1), custom_call_target="tpu_custom_call" | custom-call | tf_op jit(solution)/shard_map/attention_and_weight_grad/pallas_call | solution.py:342
  90.0 0.0 copy-start
  90.0 2.3 %copy.10 = bf16[128,4096]{1,0:T(8,128)(2,1)} copy(bf16[128,4096]{1,0:T(8,128)(2,1)} %get-tuple-element.4) | data formatting | bytes 2097152
  92.3 0.0 copy-done
  92.3 0.6 copy.11
Async XLA Ops:
  90.0 2.3 %copy-start = (f32[8,1024]{1,0:T(8,128)S(1)}, f32[8,1024]{1,0:T(8,128)}, u32[]{:S(2)}) copy-start(f32[8,1024]{1,0:T(8,128)} %get-tuple-element.5) | copy-start | bytes 98308

commit v3 on v2

--- a/solution.py
+++ b/solution.py
@@ -16,15 +16,18 @@
 LOG2E = 1.4426950408889634
 HIDDEN = -1e30
 
-IN0, IN1, IN2, ATT, OUT2, OUT3, OUT4, MUL, SUMY, SUMZ = 0, 1, 2, 3, 5, 6, 7, 9, 12, 14
+IN1, IN2, SEND_X, ATT = 0, 1, 1, 3
+OUT2, OUT3, OUT4, MATE, MUL, SUMY, SUMZ = 7, 9, 11, 13, 15, 19, 22
 STEPS = 2 * HEADS - 1 + SUMZ
 HALF = MEMBERS // 2
 
 
 def kernel(
     doc_hbm, q_hbm, k_hbm, v_hbm, og_hbm, x_ref, dq_hbm, w_ref,
-    doc_ref, q_ref, og_ref, dq_ref, kv, bias, parts, osend, orecv, rows, xin, wsend, yrecv, zsend, zrecv,
-    load_s, kv_s, dq_s, in_s, in_r, out_s, out_r, x_s, x_r, x_own, ag_s, ag_r, y_s, y_r, z_s, z_r,
+    doc_ref, q_ref, og_ref, dq_ref, kv, bias, parts, osend, orecv, rows, xin, ksend, krecv, vsend, vrecv,
+    ksum, klast, vsum, vlast,
+    load_s, kv_s, dq_s, in_s, in_r, out_s, out_r, x_s, x_r, x_own, ag_s, ag_r, mate_s, mate_r, y_s, y_r, z_s, z_r,
+    y2_s, y2_r, z2_s, z2_r,
 ):
     f32, bf16 = jnp.float32, jnp.bfloat16
     attn, dp = lax.axis_index("attn"), lax.axis_index("dp")
@@ -101,10 +104,10 @@
 
     pl.semaphore_wait(barrier, 2 + 7 * 3)
 
-    def at(t, delay, body):
+    def at(t, delay, body, every=2):
         late = t - delay
-        due = (late >= 0) & (late < 2 * HEADS) & (lax.rem(late + 2, 2) == 0)
-        pl.when(due)(lambda: body(jnp.clip(late // 2, 0, HEADS - 1)))
+        due = (late >= 0) & (late < every * HEADS) & (lax.rem(late + 2, every) == 0)
+        pl.when(due)(lambda: body(jnp.clip(late // every, 0, HEADS - 1)))
 
     def pass_in(g, o):
         return remote(kv.at[g, o], kv.at[g, o + 1], in_s.at[g, o], in_r.at[g, o], right)
@@ -196,7 +199,21 @@
         pass_out(g, 2).start()
 
     def share_rows(g, r):
-        return remote(rows.at[g, 0], rows.at[g, r], ag_s.at[g], ag_r.at[g], in_team(r))
+        return remote(rows.at[g, 0], rows.at[g, r], ag_s.at[g], ag_r.at[g, r], in_team(r))
+
+    def share_mate(g):
+        return remote(
+            rows.at[g, pl.ds(1, NX - 1)], rows.at[g, pl.ds(NX + 1, NX - 1)],
+            mate_s.at[g], mate_r.at[g], in_team(NX),
+        )
+
+    def do_mate(g):
+        def receive(r, carry):
+            share_rows(g, r).wait_recv()
+            return carry
+
+        lax.fori_loop(1, NX, receive, 0)
+        share_mate(g).start()
 
     def do_out4(g):
         pass_out(g, 2).wait_recv()
@@ -206,60 +223,82 @@
             share_rows(g, r).start()
             return carry
 
-        lax.fori_loop(1, 8, send, 0)
+        lax.fori_loop(1, NX + 1, send, 0)
 
     def share_y(g, s):
         return remote(
-            wsend.at[g, lax.rem(y + s, NY)], yrecv.at[g, s - 1], y_s.at[g], y_r.at[g], in_y(s)
+            ksend.at[g, lax.rem(y + s, NY)], krecv.at[g, s - 1], y_s.at[g], y_r.at[g], in_y(s)
+        )
+
+    def share_z(g, s):
+        return remote(
+            vsend.at[g, lax.rem(z + s, NZ)], vrecv.at[g, s - 1], z_s.at[g], z_r.at[g], in_z(s)
+        )
+
+    def last_z(g, s):
+        return remote(
+            ksum.at[g, lax.rem(z + s, NZ)], klast.at[g, s - 1], z2_s.at[g], z2_r.at[g], in_z(s)
+        )
+
+    def last_y(g, s):
+        return remote(
+            vsum.at[g, lax.rem(y + s, NY)], vlast.at[g, s - 1], y2_s.at[g], y2_r.at[g], in_y(s)
         )
 
     def do_mul(g):
-        arrived(rows.at[g, pl.ds(1, 7)], ag_r.at[g])
+        share_rows(g, NX).wait_recv()
+        share_mate(g).wait_recv()
         taken = jnp.concatenate(
             [xin[r].reshape(NY * 64, TOK) for r in range(8)], axis=1
         )
         out = jnp.dot(taken, rows[g].reshape(8 * TOK, 2 * DH), preferred_element_type=f32)
-        wsend[g] = out.astype(bf16).reshape(NY, 64, 2 * DH)
+        ksend[g] = out[:, :DH].astype(bf16).reshape(NY, 64, DH)
+        by_z = [out[(i * NZ + k) * 8:(i * NZ + k + 1) * 8, DH:] for k in range(NZ) for i in range(NY)]
+        vsend[g] = jnp.concatenate(by_z, axis=0).astype(bf16).reshape(NZ, 64, DH)
 
         def send(s, carry):
             share_y(g, s).start()
-            return carry
-
-        lax.fori_loop(1, NY, send, 0)
-
-    def share_z(g, s):
-        return remote(
-            zsend.at[g, lax.rem(z + s, NZ)], zrecv.at[g, s - 1], z_s.at[g], z_r.at[g], in_z(s)
-        )
-
-    def do_sumy(g):
-        arrived(yrecv.at[g], y_r.at[g])
-        total = wsend[g, y].astype(f32)
-        for s in range(NY - 1):
-            total = total + yrecv[g, s].astype(f32)
-        zsend[g] = total.reshape(NZ, 8, 2 * DH)
-
-        def send(s, carry):
             share_z(g, s).start()
             return carry
 
+        lax.fori_loop(1, NY, send, 0)
+
+    def do_sumy(g):
+        arrived(krecv.at[g], y_r.at[g])
+        total = ksend[g, y].astype(f32)
+        for s in range(NY - 1):
+            total = total + krecv[g, s].astype(f32)
+        ksum[g] = total.reshape(NZ, 8, DH)
+        arrived(vrecv.at[g], z_r.at[g])
+        total = vsend[g, z].astype(f32)
+        for s in range(NZ - 1):
+            total = total + vrecv[g, s].astype(f32)
+        vsum[g] = total.reshape(NY, 8, DH)
+
+        def send(s, carry):
+            last_z(g, s).start()
+            last_y(g, s).start()
+            return carry
+
         lax.fori_loop(1, NZ, send, 0)
 
     norm = (NX * NY * NZ * 2 * TOK) ** -0.5
 
     def do_sumz(g):
-        arrived(zrecv.at[g], z_r.at[g])
-        total = zsend[g, z]
+        arrived(klast.at[g], z2_r.at[g])
+        arrived(vlast.at[g], y2_r.at[g])
+        key_total, value_total = ksum[g, z], vsum[g, y]
         for s in range(NZ - 1):
-            total = total + zrecv[g, s]
-        total = total * norm
-        w_ref[:, pl.ds(pl.multiple_of(g * DH, DH), DH)] = total[:, :DH]
-        w_ref[:, pl.ds(pl.multiple_of((HEADS + g) * DH, DH), DH)] = total[:, DH:]
+            key_total = key_total + klast[g, s]
+            value_total = value_total + vlast[g, s]
+        w_ref[:, pl.ds(pl.multiple_of(g * DH, DH), DH)] = key_total * norm
+        w_ref[:, pl.ds(pl.multiple_of((HEADS + g) * DH, DH), DH)] = value_total * norm
 
     def step(t, carry):
-        at(t, IN0, do_in0)
-
-        @pl.when(t == 0)
+        at(t, IN1, do_in1, 1)
+        at(t, IN2, do_in2, 1)
+
+        @pl.when(t == SEND_X)
         def _():
             own_x.start()
 
@@ -269,11 +308,10 @@
 
             lax.fori_loop(1, 8, send, 0)
 
-        at(t, IN1, do_in1)
-        at(t, IN2, do_in2)
         at(t, OUT2, do_out2)
         at(t, OUT3, do_out3)
         at(t, OUT4, do_out4)
+        at(t, MATE, do_mate)
 
         @pl.when(t == MUL)
         def _():
@@ -309,6 +347,11 @@
 
         return carry
 
+    def start_in(g, carry):
+        do_in0(g)
+        return carry
+
+    lax.fori_loop(0, HEADS, start_in, 0)
     lax.fori_loop(0, STEPS, step, 0)
 
     def sent_x(r, carry):
@@ -321,9 +364,12 @@
         for o in range(SPAN):
             pass_in(g, o).wait_send()
             pass_out(g, o).wait_send()
-        arrived(rows.at[g, pl.ds(1, 7)], ag_s.at[g])
-        arrived(yrecv.at[g], y_s.at[g])
-        arrived(zrecv.at[g], z_s.at[g])
+        arrived(rows.at[g, pl.ds(1, NX)], ag_s.at[g])
+        share_mate(g).wait_send()
+        arrived(krecv.at[g], y_s.at[g])
+        arrived(vrecv.at[g], z_s.at[g])
+        arrived(klast.at[g], z2_s.at[g])
+        arrived(vlast.at[g], y2_s.at[g])
         leave_dq(g, 0).wait()
         leave_dq(g, 1).wait()
         return carry
@@ -359,17 +405,23 @@
             pltpu.VMEM((HEADS, SPAN, TOK, 2 * DH), bf16),
             pltpu.VMEM((HEADS, 8, TOK, 2 * DH), bf16),
             pltpu.VMEM((8, NY, 64, TOK), bf16),
-            pltpu.VMEM((HEADS, NY, 64, 2 * DH), bf16),
-            pltpu.VMEM((HEADS, NY - 1, 64, 2 * DH), bf16),
-            pltpu.VMEM((HEADS, NZ, 8, 2 * DH), f32),
-            pltpu.VMEM((HEADS, NZ - 1, 8, 2 * DH), f32),
+            pltpu.VMEM((HEADS, NY, 64, DH), bf16),
+            pltpu.VMEM((HEADS, NY - 1, 64, DH), bf16),
+            pltpu.VMEM((HEADS, NZ, 64, DH), bf16),
+            pltpu.VMEM((HEADS, NZ - 1, 64, DH), bf16),
+            pltpu.VMEM((HEADS, NZ, 8, DH), f32),
+            pltpu.VMEM((HEADS, NZ - 1, 8, DH), f32),
+            pltpu.VMEM((HEADS, NY, 8, DH), f32),
+            pltpu.VMEM((HEADS, NY - 1, 8, DH), f32),
             dma((3,)), dma((HEADS, 2)), dma((HEADS, 2)),
             dma((HEADS, SPAN)), dma((HEADS, SPAN)),
             dma((HEADS, SPAN)), dma((HEADS, SPAN)),
             dma((8,)), dma((8,)), dma,
+            dma((HEADS,)), dma((HEADS, NX + 1)),
             dma((HEADS,)), dma((HEADS,)),
             dma((HEADS,)), dma((HEADS,)),
             dma((HEADS,)), dma((HEADS,)),
+            dma((HEADS,)), dma((HEADS,)), dma((HEADS,)), dma((HEADS,)),
         ],
         compiler_params=pltpu.CompilerParams(
             collective_id=0, has_side_effects=True, vmem_limit_bytes=62 << 20

time: 93.2 us -> 86.7 us (0.930)
  Pallas kernels: 89.3 us -> 83 us
    pallas_call x1, Pallas kernels: 89.3 us -> 83 us  [shards(): pl.pallas_call(kernel, out_shape=(jax.ShapeDtypeStruct((rows_dev, width),...]
where the time goes in v3:
time: 86.7 us; the launch traced here: 86.6 us
  Pallas kernels  83 us (96%)
  local copies, waits for them, and re-layouts  2.91 us (3%)
    pallas_call x1, Pallas kernels, shards(): pl.pallas_call(kernel, out_shape=(jax.ShapeDtypeStruct((rows_dev, width),...  83 us
    unnamed x4, local copies, waits for them, and re-layouts  2.91 us

profile of v3, /device:TPU:1, one launch (start us, length us, event | category | flops | bytes accessed | tf_op | source)
XLA Modules:
  0.0 86.6 jit_solution(16890278392551696461)
XLA Ops:
  0.6 83.0 %attention_and_weight_grad.1 = (bf16[128,4096]{1,0:T(8,128)(2,1)}, f32[8,1024]{1,0:T(8,128)}) custom-call(s32[1,12]{1,0:T(1,128)} %doc_hbm.1, bf16[128,4096]{1,0:T(8,128)(2,1)} %q_hbm.1, bf16[128,512]{1,0:T(8,128)(2,1)} %k_hbm.1, bf16[128,512]{1,0:T(8,128)(2,1)} %v_hbm.1, bf16[128,4096]{1,0:T(8,128)(2,1)} %og_hbm.1, bf16[8,8,64,128]{3,2,1,0:T(8,128)(2,1)} %bitcast.1), custom_call_target="tpu_custom_call" | custom-call | tf_op jit(solution)/shard_map/attention_and_weight_grad/pallas_call | solution.py:388
  83.6 0.0 copy-start
  83.7 2.3 %copy.10 = bf16[128,4096]{1,0:T(8,128)(2,1)} copy(bf16[128,4096]{1,0:T(8,128)(2,1)} %get-tuple-element.4) | data formatting | bytes 2097152
  86.0 0.0 copy-done
  86.0 0.6 copy.11
Async XLA Ops:
  83.6 2.3 %copy-start = (f32[8,1024]{1,0:T(8,128)S(1)}, f32[8,1024]{1,0:T(8,128)}, u32[]{:S(2)}) copy-start(f32[8,1024]{1,0:T(8,128)} %get-tuple-element.5) | copy-start | bytes 98308

commit v4 on v3

--- a/solution.py
+++ b/solution.py
@@ -257,6 +257,7 @@
         vsend[g] = jnp.concatenate(by_z, axis=0).astype(bf16).reshape(NZ, 64, DH)
 
         def send(s, carry):
+            s = lax.rem(s * 3, NY)
             share_y(g, s).start()
             share_z(g, s).start()
             return carry
@@ -276,6 +277,7 @@
         vsum[g] = total.reshape(NY, 8, DH)
 
         def send(s, carry):
+            s = lax.rem(s * 3, NZ)
             last_z(g, s).start()
             last_y(g, s).start()
             return carry

time: 86.7 us -> 86.5 us (level)
  no operation moved by 1% of the time
where the time goes in v4:
time: 86.5 us; the launch traced here: 86.3 us
  Pallas kernels  82.8 us (96%)
  local copies, waits for them, and re-layouts  2.91 us (3%)
    pallas_call x1, Pallas kernels, shards(): pl.pallas_call(kernel, out_shape=(jax.ShapeDtypeStruct((rows_dev, width),...  82.8 us
    unnamed x4, local copies, waits for them, and re-layouts  2.91 us

profile of v4, /device:TPU:1, one launch (start us, length us, event | category | flops | bytes accessed | tf_op | source)
XLA Modules:
  0.0 86.3 jit_solution(4646115787459818054)
XLA Ops:
  0.6 82.8 %attention_and_weight_grad.1 = (bf16[128,4096]{1,0:T(8,128)(2,1)}, f32[8,1024]{1,0:T(8,128)}) custom-call(s32[1,12]{1,0:T(1,128)} %doc_hbm.1, bf16[128,4096]{1,0:T(8,128)(2,1)} %q_hbm.1, bf16[128,512]{1,0:T(8,128)(2,1)} %k_hbm.1, bf16[128,512]{1,0:T(8,128)(2,1)} %v_hbm.1, bf16[128,4096]{1,0:T(8,128)(2,1)} %og_hbm.1, bf16[8,8,64,128]{3,2,1,0:T(8,128)(2,1)} %bitcast.1), custom_call_target="tpu_custom_call" | custom-call | tf_op jit(solution)/shard_map/attention_and_weight_grad/pallas_call | solution.py:390
  83.4 0.0 copy-start
  83.4 2.3 %copy.10 = bf16[128,4096]{1,0:T(8,128)(2,1)} copy(bf16[128,4096]{1,0:T(8,128)(2,1)} %get-tuple-element.4) | data formatting | bytes 2097152
  85.7 0.0 copy-done
  85.7 0.6 copy.11
Async XLA Ops:
  83.4 2.3 %copy-start = (f32[8,1024]{1,0:T(8,128)S(1)}, f32[8,1024]{1,0:T(8,128)}, u32[]{:S(2)}) copy-start(f32[8,1024]{1,0:T(8,128)} %get-tuple-element.5) | copy-start | bytes 98308
